TPU v7x, 256 devices: a whole 4x4x8 slice. The times are simulated.
256 devices in a mesh: dp: 32 (over y, z), mp: 8 (over x, core).
Axes of the slice: x: 4, y: 4, z: 8, core: 2. Of those that a mesh axis runs over, the one named last changes fastest.
Arguments:
- tokens: bfloat16 [8192, 2048], P('dp'), may hold values from -6 to 6
- out_grad: bfloat16 [8192, 2048], P('dp'), may hold values from -6 to 6
- master: float32 [2240, 3, 7168], P('dp', None, 'mp'), may hold values from -6 to 6
- moment_one: float32 [2240, 3, 7168], P('dp', None, 'mp'), may hold values from -6 to 6
- moment_two: float32 [2240, 3, 7168], P('dp', None, 'mp'), may hold values from 0.05 to 5
- old_offsets: int32 [33], replicated, may hold values from 0 to 2048, as said below
- new_offsets: int32 [33], replicated, may hold values from 0 to 2048, as said below
Outputs:
- new_master: float32 [2752, 3, 7168], P('dp', None, 'mp')
- new_moment_one: float32 [2752, 3, 7168], P('dp', None, 'mp')
- new_moment_two: float32 [2752, 3, 7168], P('dp', None, 'mp')
- layer_output: bfloat16 [8192, 2048], P('dp', 'mp')
Inputs may be any that keep to these rules, and one draw needn't show every extreme that they name: non-decreasing, old_offsets[0] = 0 and old_offsets[32] = 2048; device p holds rows old_offsets[p] to old_offsets[p + 1] - 1 in its first slots; every device holds at least one and at most 70 rows, and some device exactly 70. non-decreasing, new_offsets[0] = 0 and new_offsets[32] = 2048; exactly one device holds no rows, its index at least 2 and at most 15; every other device holds at least one and at most 86 rows, some device exactly 86; a row's device in the new layout is its device in the old layout or the next one along dp.
All inputs are finite; a program needn't handle non-finite values.
Results may differ from a plain program's by a relative error of at most 0.014.
Values may be sent and summed in bfloat16 or wider, within the bound.
No kernel may reach another device: no remote copies, remote signals or barrier semaphores. Data moves between devices by JAX's collectives and lax.ppermute only.
A program may use at most 128 MiB of HBM per device.

v0:
```python
import jax
import jax.numpy as jnp
from jax import lax
from jax.sharding import PartitionSpec as P

FEATURE_WIDTH = 2048
FF = 7168
beta_one = 0.9
beta_two = 0.95
learn_rate = 0.01
decay_rate = 0.1
adam_eps = 1e-08
bias_one = 1.0 - 0.9**10
bias_two = 1.0 - 0.95**10


def passed_along(value, axis, by):
    peers = lax.axis_size(axis)
    pairs = [(i, i + by) for i in range(peers) if 0 <= i + by < peers]
    return lax.ppermute(value, axis, pairs)


def lookup(small_table, wanted):
    matches = wanted[..., None] == jnp.arange(small_table.shape[0], dtype=jnp.int32)
    return jnp.sum(jnp.where(matches, small_table, 0), axis=-1)


def row_layout(row_count, capacity, offsets):
    row_index = jnp.arange(row_count, dtype=jnp.int32)
    owner_index = row_index // capacity
    local_index = row_index - owner_index * capacity
    row_start = lookup(offsets, owner_index)
    in_range = local_index < lookup(offsets, owner_index + 1) - row_start
    target = jnp.clip(row_start + local_index, 0, FEATURE_WIDTH - 1)
    return (target, in_range)


def adam_step(master_rows, first_rows, second_rows, grads):
    first_new = beta_one * first_rows + (1.0 - beta_one) * grads
    second_new = beta_two * second_rows + (1.0 - beta_two) * grads * grads
    update = first_new / bias_one / (jnp.sqrt(second_new / bias_two) + adam_eps)
    master_new = master_rows - learn_rate * (update + decay_rate * master_rows)
    return (master_new, first_new, second_new)


def reshard(states, old_offsets, new_offsets, capacity_new):
    capacity_old = states.shape[0]
    from_left = passed_along(states.astype(jnp.bfloat16), "dp", 1).astype(states.dtype)
    device_index = lax.axis_index("dp")
    local_index = jnp.arange(capacity_new, dtype=jnp.int32)
    row_start = lookup(new_offsets, device_index)
    row_count = lookup(new_offsets, device_index + 1) - row_start
    in_range = local_index < row_count
    row_index = jnp.clip(row_start + local_index, 0, FEATURE_WIDTH - 1)
    owner_index = jnp.sum(
        (old_offsets[1:-1][None, :] <= row_index[:, None]).astype(jnp.int32), axis=1
    )
    slot_index = (
        (owner_index - device_index + 1) * capacity_old
        + row_index
        - lookup(old_offsets, owner_index)
    )
    neighbours = jnp.concatenate([from_left, states], axis=0)
    picked = jnp.take(neighbours, slot_index, axis=0, mode="clip")
    return jnp.where(in_range[:, None, None, None], picked, 0.0)


def train_pass(tokens, upstream, weights, layout, capacity, live_flag):
    columns = weights.shape[2]
    scale_in = FEATURE_WIDTH ** (-0.5)
    scale_hidden = FF ** (-0.5)
    contract_rows = (((0,), (0,)), ((), ()))
    shard_piece = lax.all_gather(weights, "dp", axis=0, tiled=True)
    down_rows = jnp.zeros((FEATURE_WIDTH, columns), jnp.bfloat16)
    target, in_range = row_layout(shard_piece.shape[0], capacity, layout)
    shard_piece = jnp.where(in_range[:, None, None], shard_piece, jnp.zeros_like(shard_piece))
    token_columns = jnp.take(tokens, target, axis=1, mode="clip")
    upstream_columns = jnp.take(upstream, target, axis=1, mode="clip")
    gate_sum = jnp.dot(token_columns, shard_piece[:, 0], preferred_element_type=jnp.float32)
    up_sum = jnp.dot(token_columns, shard_piece[:, 1], preferred_element_type=jnp.float32)
    back_sum = jnp.dot(upstream_columns, shard_piece[:, 2], preferred_element_type=jnp.float32)
    placed = jnp.where(in_range, target, FEATURE_WIDTH)
    down_rows = down_rows.at[placed].set(shard_piece[:, 2], mode="drop")
    gate_sum, up_sum, back_sum, down_rows = (gate_sum, up_sum, back_sum, down_rows)
    gate_act = gate_sum * scale_in
    up_act = up_sum * scale_in
    back_grad = back_sum * scale_hidden
    sigmoid_gate = jax.nn.sigmoid(gate_act)
    hidden = (gate_act * sigmoid_gate * up_act).astype(jnp.bfloat16)
    partial_value = (
        lax.dot_general(
            hidden, down_rows, (((1,), (1,)), ((), ())), preferred_element_type=jnp.float32
        )
        * scale_hidden
    )
    partial_value = jnp.where(live_flag, partial_value, 0.0)
    layer_output = lax.psum_scatter(
        partial_value.astype(jnp.bfloat16), "mp", scatter_dimension=1, tiled=True
    )
    gate_grad = (
        back_grad * up_act * sigmoid_gate * (1.0 + gate_act * (1.0 - sigmoid_gate))
    ).astype(jnp.bfloat16)
    up_grad = (back_grad * gate_act * sigmoid_gate).astype(jnp.bfloat16)
    target, in_range = row_layout(lax.axis_size("dp") * capacity, capacity, layout)
    token_columns = jnp.take(tokens, target, axis=1, mode="clip")
    upstream_columns = jnp.take(upstream, target, axis=1, mode="clip")
    gate_part = (
        lax.dot_general(token_columns, gate_grad, contract_rows, preferred_element_type=jnp.float32)
        * scale_in
    )
    up_part = (
        lax.dot_general(token_columns, up_grad, contract_rows, preferred_element_type=jnp.float32)
        * scale_in
    )
    down_part = (
        lax.dot_general(upstream_columns, hidden, contract_rows, preferred_element_type=jnp.float32)
        * scale_hidden
    )
    stacked = jnp.stack([gate_part, up_part, down_part], axis=1)
    grads = lax.psum_scatter(
        jnp.where(in_range[:, None, None], stacked, 0.0).astype(jnp.bfloat16),
        "dp",
        scatter_dimension=0,
        tiled=True,
    ).astype(jnp.float32)
    return (grads, layer_output)


def body(tokens, out_grad, master, moment_one, moment_two, old_offsets, new_offsets):
    devices = lax.axis_size("dp")
    shard_rows = FEATURE_WIDTH // devices
    jitter_rows = shard_rows // (2 * (devices - 1)) + 2
    capacity_new = shard_rows + shard_rows // 4 + 2 * jitter_rows
    device_index = lax.axis_index("dp")
    live_flag = lookup(new_offsets, device_index + 1) != lookup(new_offsets, device_index)
    upstream = jnp.where(live_flag, out_grad, jnp.zeros_like(out_grad))
    states = jnp.stack([master, moment_one, moment_two], axis=1)
    states = reshard(states, old_offsets, new_offsets, capacity_new)
    weights = states[:, 0].astype(jnp.bfloat16)
    grads, layer_output = train_pass(
        tokens, upstream, weights, new_offsets, states.shape[0], live_flag
    )
    updated = jnp.stack(adam_step(states[:, 0], states[:, 1], states[:, 2], grads), axis=1)
    return (updated[:, 0], updated[:, 1], updated[:, 2], layer_output)


def solution(mesh):
    placed = (
        P("dp", None),
        P("dp", None),
        P("dp", None, "mp"),
        P("dp", None, "mp"),
        P("dp", None, "mp"),
        P(),
        P(),
    )
    return jax.shard_map(
        body,
        mesh=mesh,
        in_specs=placed,
        out_specs=(P("dp", None, "mp"), P("dp", None, "mp"), P("dp", None, "mp"), P("dp", "mp")),
        check_vma=False,
    )
```

profile of v0, /device:TPU:8, one launch (start us, length us, event | category | flops | bytes accessed | tf_op | source)
XLA Modules:
  0.0 586.7 jit_solution(979489931884639020)
XLA Ops:
  7.2 3.0 maximum_convert_fusion
  10.2 3.8 collective-permute-start
  14.1 0.7 slice.23
  14.8 1.3 fusion.27
  18.1 0.7 select_reduce_fusion.2
  19.6 24.1 %collective-permute-done = bf16[70,3,3,896]{3,0,2,1:T(8,128)(2,1)S(1)} collective-permute-done((bf16[70,3,3,896]{3,0,2,1:T(8,128)(2,1)}, bf16[70,3,3,896]{3,0,2,1:T(8,128)(2,1)S(1)}, u32[]{:S(2)}, u32[]{:S(2)}) %collective-permute-start) | collective-permute-done | bytes 1128992 | tf_op jit(solution)/shard_map/ppermute | solution.py:20
  44.2 4.9 copy.47
  49.1 7.4 %gather_fusion = f32[86,3,3,896]{3,2,1,0:T(4,128)} fusion(f32[140,3,3,896]{3,2,1,0:T(4,128)} %copy.47, s32[1024]{0:T(1024)S(1)} %pad_clamp_fusion.1), kind=kCustom, calls=%fused_computation | custom fusion | bytes 5548376 | tf_op jit(solution)/shard_map/jit(_take)/gather | solution.py:64
  56.6 3.0 broadcast_select_fusion
  59.6 1.9 copy-done.1
  61.5 1.0 fusion.16
  65.5 8.8 %gather_fusion.1 = bf16[2752,256]{1,0:T(8,128)(2,1)} fusion(bf16[256,2048]{0,1:T(8,128)(2,1)S(1)} %copy.50, s32[3072]{0:T(1024)S(1)} %pad_clamp_fusion), kind=kCustom, calls=%fused_computation.1 | custom fusion | bytes 2829056 | tf_op jit(solution)/shard_map/jit(_take)/gather | solution.py:105
  74.3 8.5 %gather_fusion.2 = bf16[2752,256]{1,0:T(8,128)(2,1)S(1)} fusion(bf16[256,2048]{0,1:T(8,128)(2,1)S(1)} %copy.51, s32[3072]{0:T(1024)S(1)} %pad_clamp_fusion), kind=kCustom, calls=%fused_computation.2 | custom fusion | bytes 2829056 | tf_op jit(solution)/shard_map/jit(_take)/gather | solution.py:78
  82.9 134.0 %all-gather.2.cloned.1.call-done = bf16[2752,3,896]{2,1,0:T(4,128)(2,1)} async-done(((bf16[86,3,896]{2,1,0:T(4,128)(2,1)}), bf16[2752,3,896]{2,1,0:T(4,128)(2,1)}) %all-gather.2.cloned.1.call-update) | async-done | bytes 14794768 | tf_op jit(solution)/shard_map/all_gather | solution.py:73
  216.8 12.4 %copy_select_fusion = bf16[2752,3,896]{2,0,1:T(8,128)(2,1)S(1)} fusion(bf16[2752,3,896]{2,1,0:T(4,128)(2,1)} %all-gather.2.cloned.1.call-done, pred[2752]{0:T(1024)(128)(4,1)S(1)} %fusion.21), kind=kLoop, calls=%fused_computation.6 | loop fusion | flops 7397376 | bytes 29592256 | tf_op jit(solution)/shard_map/jit(_where)/select_n | solution.py:76
  229.2 1.7 fusion.10
  230.9 1.8 multiply_convert_fusion
  232.8 1.7 copy-done
  234.5 1.7 fusion.8
  236.2 1.8 multiply_bitcast_fusion.1
  238.0 1.8 multiply_bitcast_fusion.2
  239.8 1.6 multiply_bitcast_fusion
  241.4 7.7 %fusion = bf16[2752,3,896]{2,0,1:T(8,128)(2,1)} fusion(bf16[2752,1,896]{2,0,1:T(8,128)(2,1)S(1)} %multiply_bitcast_fusion, bf16[2752,1,896]{2,0,1:T(8,128)(2,1)S(1)} %multiply_bitcast_fusion.1, bf16[2752,1,896]{2,0,1:T(8,128)(2,1)S(1)} %multiply_bitcast_fusion.2, pred[2752]{0:T(1024)(128)(4,1)S(1)} %fusion.21), kind=kLoop, calls=%fused_computation.5 | loop fusion | flops 51781632 | bytes 29592256 | tf_op jit(solution)/shard_map/convert_element_type | solution.py:121
  249.2 18.7 %scatter_custom_fusion = bf16[2048,896]{1,0:T(8,128)(2,1)} fusion(s32[2752]{0:T(1024)S(1)} %get-tuple-element.16, bf16[2752,3,896]{2,0,1:T(8,128)(2,1)} %copy-done, bf16[]{:T(256)} %constant.32.clone.1), kind=kCustom, calls=%fused_computation.16 | custom fusion | bytes 8602112 | tf_op jit(solution)/shard_map/scatter | solution.py:83
  267.9 4.6 fusion.6
  273.8 269.6 %all-reduce.3.cloned.1.call-done = bf16[2752,3,896]{2,0,1:T(8,128)(2,1)} async-done(((bf16[2752,3,896]{2,0,1:T(8,128)(2,1)}), bf16[2752,3,896]{2,0,1:T(8,128)(2,1)}) %all-reduce.3.cloned.1.call-update) | async-done | bytes 14794768
  543.4 1.2 constant_dynamic-slice_fusion
  544.5 3.8 multiply_subtract_fusion
  548.3 1.0 copy.54
  549.3 1.0 copy.55
  550.3 1.0 copy.56
  551.3 28.9 %reduce-scatter.3.cloned.1.call-done = bf16[256,256]{1,0:T(8,128)(2,1)} async-done(((bf16[256,2048]{1,0:T(8,128)(2,1)}), bf16[256,256]{1,0:T(8,128)(2,1)}) %reduce-scatter.3.cloned.1.call-update) | async-done | bytes 131088 | tf_op jit(solution)/shard_map/reduce_scatter | solution.py:97
  (40 shorter events, 4.2 us)
Async XLA Ops:
  7.2 36.7 %copy-start.4 = (f32[70,3,896]{2,0,1:T(8,128)S(1)}, f32[70,3,896]{2,0,1:T(8,128)}, u32[]{:S(2)}) copy-start(f32[70,3,896]{2,0,1:T(8,128)} %param.9) | copy-start | bytes 2257924
  7.2 36.7 %copy-start.3 = (f32[70,3,896]{2,0,1:T(8,128)S(1)}, f32[70,3,896]{2,0,1:T(8,128)}, u32[]{:S(2)}) copy-start(f32[70,3,896]{2,0,1:T(8,128)} %param.10) | copy-start | bytes 2257924
  7.2 36.7 %copy-start.2 = (f32[70,3,896]{2,0,1:T(8,128)S(1)}, f32[70,3,896]{2,0,1:T(8,128)}, u32[]{:S(2)}) copy-start(f32[70,3,896]{2,0,1:T(8,128)} %param.11) | copy-start | bytes 2257924
  7.2 209.7 %all-gather.2.cloned.1.call-start = ((), (), s32[]{:S(2)}) async-start(), calls=%async_computation.1 | async-start | bytes 20342784 | tf_op jit(solution)/shard_map/all_gather | solution.py:73
  10.2 33.4 %collective-permute-start = (bf16[70,3,3,896]{3,0,2,1:T(8,128)(2,1)}, bf16[70,3,3,896]{3,0,2,1:T(8,128)(2,1)S(1)}, u32[]{:S(2)}, u32[]{:S(2)}) collective-permute-start(bf16[70,3,3,896]{3,0,2,1:T(8,128)(2,1)} %maximum_convert_fusion), channel_id=1, source_target_pairs={{0,8},{8,16},{16,24},{24,32},{32,40},{40,48},{48,56},{56,64},{64,7... | collective-permute-start | bytes 3386888 | tf_op jit(solution)/shard_map/ppermute | solution.py:20
  56.6 7.4 %copy-start.7 = (bf16[256,2048]{1,0:T(8,128)(2,1)S(1)}, bf16[256,2048]{1,0:T(8,128)(2,1)}, u32[]{:S(2)}) copy-start(bf16[256,2048]{1,0:T(8,128)(2,1)} %param.7) | copy-start | bytes 3145732
  59.6 1.9 copy-start.1
  61.5 3.0 copy-start.6
  62.5 2.6 copy-start.8
  62.6 480.8 %all-reduce.3.cloned.1.call-start = ((), (), s32[]{:S(2)}) async-start(), calls=%async_computation.3 | async-start | bytes 29589504
  82.9 146.3 %copy-start.5 = (bf16[2752,256]{1,0:T(8,128)(2,1)S(1)}, bf16[2752,256]{1,0:T(8,128)(2,1)}, u32[]{:S(2)}) copy-start(bf16[2752,256]{1,0:T(8,128)(2,1)} %gather_fusion.1) | copy-start | bytes 4227076
  229.2 5.3 copy-start
  249.2 331.1 %reduce-scatter.3.cloned.1.call-start = ((), (), s32[]{:S(2)}) async-start(), calls=%async_computation.2 | async-start | bytes 1179648 | tf_op jit(solution)/shard_map/reduce_scatter | solution.py:97
  267.9 4.6 copy-start.9
Sparse Core Ops, SparseCore 0:
  62.7 154.1 all-gather.1
  249.3 294.0 all-reduce.2
  546.5 33.7 reduce-scatter.2
where the time goes:
time: 587 us
  waiting for transfers between devices  457 us (78%)
  local copies, waits for them, and re-layouts  59.7 us (10%)
  other arithmetic  34.3 us (6%)
  between operations  17.3 us (3%)
  matrix products  15 us (3%)
    unnamed x4, waiting for transfers between devices  270 us
    all_gather x1, waiting for transfers between devices, train_pass(): shard_piece = lax.all_gather(weights, 'dp', axis=0, tiled=True)  134 us
    reduce_scatter x1, waiting for transfers between devices, train_pass(): lax.psum_scatter(partial_value.astype(jnp.bfloat16), 'mp', scatter_dimens...  28.9 us
    ppermute x1, waiting for transfers between devices, passed_along(): return lax.ppermute(value, axis, pairs)  24.1 us
    scatter x1, local copies, waits for them, and re-layouts, train_pass(): down_rows = down_rows.at[placed].set(shard_piece[:, 2], mode='drop')  18.7 us
    select_n x1, other arithmetic, train_pass(): jnp.where(in_range[:, None, None], shard_piece, jnp.zeros_like(shard_piece))  12.4 us
  transfers between devices with their start and end apart: 4, of which 4 were waited for; matrix products, arithmetic and copies ran while one was open for 9% of the time, Pallas kernels for 0%

commit v1 on v0

--- a/solution.py
+++ b/solution.py
@@ -70,7 +70,10 @@
     scale_in = FEATURE_WIDTH ** (-0.5)
     scale_hidden = FF ** (-0.5)
     contract_rows = (((0,), (0,)), ((), ()))
-    shard_piece = lax.all_gather(weights, "dp", axis=0, tiled=True)
+    devices_2 = lax.axis_size("dp")
+    blocks = jnp.stack([weights for _ in range(devices_2)])
+    blocks = lax.all_to_all(blocks, "dp", split_axis=0, concat_axis=0)
+    shard_piece = jnp.concatenate(blocks, axis=0)
     down_rows = jnp.zeros((FEATURE_WIDTH, columns), jnp.bfloat16)
     target, in_range = row_layout(shard_piece.shape[0], capacity, layout)
     shard_piece = jnp.where(in_range[:, None, None], shard_piece, jnp.zeros_like(shard_piece))

time: 587 us -> 812 us (1.38)
  waiting for transfers between devices: 457 us -> 634 us
  local copies, waits for them, and re-layouts: 59.7 us -> 98.5 us
  starting transfers between devices: 3.93 us -> 13.2 us
    all_to_all x0 -> x1, waiting for transfers between devices: none -> 324 us  [train_pass(): blocks = lax.all_to_all(blocks, 'dp', split_axis=0, concat_axis=0)]
    all_gather x1 -> x0, waiting for transfers between devices: 134 us -> none  [train_pass(): shard_piece = lax.all_gather(weights, 'dp', axis=0, tiled=True)]
    reduce_scatter x1, waiting for transfers between devices: 28.9 us -> 0.01 us  [train_pass(): lax.psum_scatter(partial_value.astype(jnp.bfloat16), 'mp', scatter_dimens...]
    reshape x0 -> x1, local copies, waits for them, and re-layouts: none -> 19.6 us  [train_pass(): shard_piece = jnp.concatenate(blocks, axis=0)]
    unnamed x4 -> x3, waiting for transfers between devices: 270 us -> 287 us
    all_to_all x0 -> x1, local copies, waits for them, and re-layouts: none -> 13.6 us  [train_pass(): blocks = lax.all_to_all(blocks, 'dp', split_axis=0, concat_axis=0)]
    all_to_all x0 -> x1, starting transfers between devices: none -> 9.09 us  [train_pass(): blocks = lax.all_to_all(blocks, 'dp', split_axis=0, concat_axis=0)]
  transfers between devices with their start and end apart: 4 -> 4, of which waited for: 4 -> 3; matrix products, arithmetic and copies ran while one was open for 9% -> 7% of each run, Pallas kernels for 0% -> 0%
where the time goes in v1:
time: 812 us; the launch traced here: 810 us
  waiting for transfers between devices  634 us (78%)
  local copies, waits for them, and re-layouts  98.5 us (12%)
  other arithmetic  30.1 us (4%)
  between operations  19.1 us (2%)
  matrix products  14.9 us (2%)
  starting transfers between devices  13.2 us (2%)
    all_to_all x1, waiting for transfers between devices, train_pass(): blocks = lax.all_to_all(blocks, 'dp', split_axis=0, concat_axis=0)  324 us
    unnamed x3, waiting for transfers between devices  287 us
    ppermute x1, waiting for transfers between devices, passed_along(): return lax.ppermute(value, axis, pairs)  24.1 us
    reshape x1, local copies, waits for them, and re-layouts, train_pass(): shard_piece = jnp.concatenate(blocks, axis=0)  19.6 us
    scatter x1, local copies, waits for them, and re-layouts, train_pass(): down_rows = down_rows.at[placed].set(shard_piece[:, 2], mode='drop')  18.7 us
  transfers between devices with their start and end apart: 4, of which 3 were waited for; matrix products, arithmetic and copies ran while one was open for 7% of the time, Pallas kernels for 0%

profile of v1, /device:TPU:8, one launch (start us, length us, event | category | flops | bytes accessed | tf_op | source)
XLA Modules:
  0.0 810.2 jit_solution(15133640959747882339)
XLA Ops:
  8.0 3.0 maximum_convert_fusion
  11.0 3.8 collective-permute-start
  15.6 1.3 fusion.27
  20.4 24.1 %collective-permute-done = bf16[70,3,3,896]{3,0,2,1:T(8,128)(2,1)S(1)} collective-permute-done((bf16[70,3,3,896]{3,0,2,1:T(8,128)(2,1)}, bf16[70,3,3,896]{3,0,2,1:T(8,128)(2,1)S(1)}, u32[]{:S(2)}, u32[]{:S(2)}) %collective-permute-start) | collective-permute-done | bytes 1128992 | tf_op jit(solution)/shard_map/ppermute | solution.py:20
  45.0 4.9 copy.49
  49.9 7.4 gather_fusion
  57.4 2.9 broadcast_select_fusion.1
  60.3 1.9 copy-done.1
  62.5 6.5 stack.22
  68.9 9.1 %all-to-all-start = ((bf16[32,86,3,896]{3,1,2,0:T(8,128)(2,1)}), bf16[32,86,3,896]{3,1,2,0:T(8,128)(2,1)}, u32[]{:S(2)}, u32[]{:S(2)}) async-start(bf16[32,86,3,896]{3,1,2,0:T(8,128)(2,1)} %stack.22), calls=%async_computation | async-start | bytes 30277632 | tf_op jit(solution)/shard_map/all_to_all | solution.py:75
  81.1 8.9 %gather_fusion.1 = bf16[2752,256]{1,0:T(8,128)(2,1)} fusion(bf16[256,2048]{0,1:T(8,128)(2,1)S(1)} %copy.52, s32[3072]{0:T(1024)S(1)} %pad_clamp_fusion), kind=kCustom, calls=%fused_computation.1 | custom fusion | bytes 2829056 | tf_op jit(solution)/shard_map/jit(_take)/gather | solution.py:108
  90.0 8.5 %gather_fusion.2 = bf16[2752,256]{1,0:T(8,128)(2,1)S(1)} fusion(bf16[256,2048]{0,1:T(8,128)(2,1)S(1)} %copy.53, s32[3072]{0:T(1024)S(1)} %pad_clamp_fusion), kind=kCustom, calls=%fused_computation.2 | custom fusion | bytes 2829056 | tf_op jit(solution)/shard_map/jit(_take)/gather | solution.py:81
  98.5 323.9 %all-to-all-done = bf16[32,86,3,896]{3,1,2,0:T(8,128)(2,1)} async-done(((bf16[32,86,3,896]{3,1,2,0:T(8,128)(2,1)}), bf16[32,86,3,896]{3,1,2,0:T(8,128)(2,1)}, u32[]{:S(2)}, u32[]{:S(2)}) %all-to-all-start) | async-done | bytes 14794784 | tf_op jit(solution)/shard_map/all_to_all | solution.py:75
  422.4 13.6 %copy.55 = bf16[32,86,3,896]{3,1,0,2:T(8,128)(2,1)} copy(bf16[32,86,3,896]{3,1,2,0:T(8,128)(2,1)} %all-to-all-done) | data formatting | bytes 29589504 | tf_op jit(solution)/shard_map/all_to_all | solution.py:75
  436.0 19.6 %reshape.174 = bf16[2752,3,896]{2,0,1:T(8,128)(2,1)} reshape(bf16[32,86,3,896]{3,1,0,2:T(8,128)(2,1)} %copy.55) | data formatting | bytes 29589504 | tf_op jit(solution)/shard_map/reshape | solution.py:76
  455.6 8.3 %broadcast_select_fusion = bf16[2752,3,896]{2,0,1:T(8,128)(2,1)S(1)} fusion(bf16[2752,3,896]{2,0,1:T(8,128)(2,1)} %reshape.174, pred[2752]{0:T(1024)(128)(4,1)S(1)} %fusion.21), kind=kLoop, calls=%fused_computation.6 | loop fusion | flops 7397376 | bytes 29592256 | tf_op jit(solution)/shard_map/jit(_where)/select_n | solution.py:79
  463.9 1.7 fusion.10
  465.6 1.8 multiply_convert_fusion
  467.5 1.7 copy-done
  469.2 1.7 fusion.8
  470.9 1.8 multiply_bitcast_fusion.1
  472.6 1.8 multiply_bitcast_fusion.2
  474.5 1.6 multiply_bitcast_fusion
  476.1 7.7 fusion
  483.9 18.7 %scatter_custom_fusion = bf16[2048,896]{1,0:T(8,128)(2,1)} fusion(s32[2752]{0:T(1024)S(1)} %get-tuple-element.16, bf16[2752,3,896]{2,0,1:T(8,128)(2,1)} %copy-done, bf16[]{:T(256)} %constant.32.clone.1), kind=kCustom, calls=%fused_computation.16 | custom fusion | bytes 8602112 | tf_op jit(solution)/shard_map/scatter | solution.py:86
  502.6 4.5 fusion.6
  508.3 286.5 %all-reduce.3.cloned.1.call-done = bf16[2752,3,896]{2,0,1:T(8,128)(2,1)} async-done(((bf16[2752,3,896]{2,0,1:T(8,128)(2,1)}), bf16[2752,3,896]{2,0,1:T(8,128)(2,1)}) %all-reduce.3.cloned.1.call-update) | async-done | bytes 14794768
  794.8 1.2 constant_dynamic-slice_fusion
  796.0 3.8 multiply_subtract_fusion
  799.8 1.0 copy.57
  800.8 1.0 copy.58
  801.8 1.0 copy.59
  (43 shorter events, 6.1 us)
Async XLA Ops:
  8.0 36.6 %copy-start.4 = (f32[70,3,896]{2,0,1:T(8,128)S(1)}, f32[70,3,896]{2,0,1:T(8,128)}, u32[]{:S(2)}) copy-start(f32[70,3,896]{2,0,1:T(8,128)} %param.9) | copy-start | bytes 2257924
  8.0 36.6 %copy-start.3 = (f32[70,3,896]{2,0,1:T(8,128)S(1)}, f32[70,3,896]{2,0,1:T(8,128)}, u32[]{:S(2)}) copy-start(f32[70,3,896]{2,0,1:T(8,128)} %param.10) | copy-start | bytes 2257924
  8.0 36.6 %copy-start.2 = (f32[70,3,896]{2,0,1:T(8,128)S(1)}, f32[70,3,896]{2,0,1:T(8,128)}, u32[]{:S(2)}) copy-start(f32[70,3,896]{2,0,1:T(8,128)} %param.11) | copy-start | bytes 2257924
  11.0 33.4 %collective-permute-start = (bf16[70,3,3,896]{3,0,2,1:T(8,128)(2,1)}, bf16[70,3,3,896]{3,0,2,1:T(8,128)(2,1)S(1)}, u32[]{:S(2)}, u32[]{:S(2)}) collective-permute-start(bf16[70,3,3,896]{3,0,2,1:T(8,128)(2,1)} %maximum_convert_fusion), channel_id=1, source_target_pairs={{0,8},{8,16},{16,24},{24,32},{32,40},{40,48},{48,56},{56,64},{64,7... | collective-permute-start | bytes 3386888 | tf_op jit(solution)/shard_map/ppermute | solution.py:20
  60.3 1.9 copy-start.1
  68.9 10.6 %copy-start.7 = (bf16[256,2048]{1,0:T(8,128)(2,1)S(1)}, bf16[256,2048]{1,0:T(8,128)(2,1)}, u32[]{:S(2)}) copy-start(bf16[256,2048]{1,0:T(8,128)(2,1)} %param.7) | copy-start | bytes 3145732
  68.9 11.2 %copy-start.6 = (bf16[256,2048]{1,0:T(8,128)(2,1)S(1)}, bf16[256,2048]{1,0:T(8,128)(2,1)}, u32[]{:S(2)}) copy-start(bf16[256,2048]{1,0:T(8,128)(2,1)} %param.8) | copy-start | bytes 3145732
  68.9 353.5 %all-to-all-start = ((bf16[32,86,3,896]{3,1,2,0:T(8,128)(2,1)}), bf16[32,86,3,896]{3,1,2,0:T(8,128)(2,1)}, u32[]{:S(2)}, u32[]{:S(2)}) async-start(bf16[32,86,3,896]{3,1,2,0:T(8,128)(2,1)} %stack.22), calls=%async_computation | async-start | bytes 30277632 | tf_op jit(solution)/shard_map/all_to_all | solution.py:75
  78.0 2.7 copy-start.8
  78.0 716.8 %all-reduce.3.cloned.1.call-start = ((), (), s32[]{:S(2)}) async-start(), calls=%async_computation.3 | async-start | bytes 29589504
  455.6 8.3 %copy-start.5 = (bf16[2752,256]{1,0:T(8,128)(2,1)S(1)}, bf16[2752,256]{1,0:T(8,128)(2,1)}, u32[]{:S(2)}) copy-start(bf16[2752,256]{1,0:T(8,128)(2,1)} %gather_fusion.1) | copy-start | bytes 4227076
  463.9 5.3 copy-start
  483.8 318.9 %reduce-scatter.3.cloned.1.call-start = ((), (), s32[]{:S(2)}) async-start(), calls=%async_computation.2 | async-start | bytes 1179648 | tf_op jit(solution)/shard_map/reduce_scatter | solution.py:100
  502.6 4.5 copy-start.9
Sparse Core Ops, SparseCore 0:
  484.0 310.8 all-reduce.2
Sparse Core Ops, SparseCore 1:
  507.2 50.4 reduce-scatter.2
